TPU v7x, 512 devices: a whole 4x8x8 slice. The times are simulated.
512 devices in a mesh: ia: 16 (over z_lo, x, core), ja: 8 (over y), ka: 4 (over z_hi).
Axes of the slice: x: 4, y: 8, z: 8 (z_hi: 4, z_lo: 2; z = z_hi * 2 + z_lo), core: 2. Of those that a mesh axis runs over, the one named last changes fastest.
Arguments:
- tensor: float32 [512, 1024, 512], P('ia', 'ja', 'ka'), may hold values from -200 to 200
- factor_b: float32 [1024, 4, 96], P(('ja', 'ka')), may hold values from -4 to 4
- factor_c: float32 [512, 4, 96], P(('ka', 'ja')), may hold values from -4 to 4
Outputs:
- factor_a: float32 [512, 4, 96], P(('ia', 'ja', 'ka'))
- weights: float32 [4, 96], replicated
All inputs are finite; a program needn't handle non-finite values.
Results may differ from a plain program's by a relative error of at most 0.0003.
Values sent between devices are 32-bit elements; how exact they have to be, the bound alone decides.
No kernel may reach another device: no remote copies, remote signals or barrier semaphores. Data moves between devices by JAX's collectives and lax.ppermute only.
A program may use at most 64 MiB of HBM per device.

v0:
```python
import jax
import jax.numpy as jnp
from jax import lax
from jax.sharding import PartitionSpec as P

highest = lax.Precision.HIGHEST


def gram_of(rows):
    return jnp.einsum(
        "jsr,jsq->srq", rows, rows, precision=highest, preferred_element_type=jnp.float32
    )


def solve_normal(rows, gram_b, gram_c):
    columns = []
    for member in range(rows.shape[1]):
        normal_mat = gram_b[member] * gram_c[member]
        factor_l = jnp.linalg.cholesky(normal_mat)
        right_side = rows[:, member, :].T
        lower_sol = lax.linalg.triangular_solve(factor_l, right_side, left_side=True, lower=True)
        upper_sol = lax.linalg.triangular_solve(
            factor_l, lower_sol, left_side=True, lower=True, transpose_a=True
        )
        columns.append(upper_sol.T)
    return jnp.stack(columns, axis=1)


def shards(tensor, factor_b, factor_c):
    rows_i, rows_j, rows_k = tensor.shape
    starts, col_count = (factor_b.shape[1], factor_b.shape[2])
    width = starts * col_count
    c_block = lax.all_gather(factor_c, "ja", axis=0, tiled=True)
    partial_value = jnp.dot(
        tensor.reshape(rows_i * rows_j, rows_k),
        c_block.reshape(rows_k, width),
        precision=highest,
        preferred_element_type=jnp.float32,
    ).reshape(rows_i, rows_j, width)
    piece = lax.all_gather(factor_b, "ka", axis=0, tiled=True)
    gram_sum = jnp.zeros((starts, col_count, col_count), jnp.float32)
    count = piece.shape[0]
    flat_rows = piece.reshape(count, width)
    mttkrp = jnp.einsum(
        "ijr,jr->ir",
        partial_value,
        flat_rows,
        precision=highest,
        preferred_element_type=jnp.float32,
    )
    mttkrp, gram_rows = (mttkrp, gram_sum)
    gram_b, gram_c = lax.psum((gram_of(factor_b), gram_of(factor_c)), ("ja", "ka"))
    slab_rows = lax.psum_scatter(mttkrp, "ja", scatter_dimension=0, tiled=True)
    owned = lax.psum_scatter(slab_rows, "ka", scatter_dimension=0, tiled=True)
    owned = owned.reshape(owned.shape[0], starts, col_count)
    factor_raw = solve_normal(owned, gram_b, gram_c)
    squares = jnp.sum(factor_raw * factor_raw, axis=0)
    total = lax.psum(squares, ("ia", "ja", "ka"))
    row_total = rows_i * lax.axis_size("ia")
    weights = jnp.sqrt(total / row_total + 1e-06)
    return (factor_raw / weights[None], weights)


def solution(mesh):
    in_specs = (P("ia", "ja", "ka"), P(("ja", "ka"), None, None), P(("ka", "ja"), None, None))
    out_specs = (P(("ia", "ja", "ka"), None, None), P())
    return jax.shard_map(shards, mesh=mesh, in_specs=in_specs, out_specs=out_specs, check_vma=False)
```

profile of v0, /device:TPU:1, one launch (start us, length us, event | category | flops | bytes accessed | tf_op | source)
XLA Modules:
  0.0 503.4 jit_solution(228719153162087754)
XLA Ops:
  7.2 0.0 copy-start
  7.2 0.0 all-reduce.5.cloned.1.call-start
  7.2 2.1 fusion.22
  9.3 2.1 fusion
  11.4 0.0 all-reduce.5.cloned.1.call-update
  11.4 18.7 %all_gather.7 = f32[128,4,96]{2,1,0:T(4,128)S(1)} all-gather(f32[32,4,96]{2,1,0:T(4,128)} %param.9), channel_id=1, replica_groups=mesh['ia'=16,'ja'=8,'ka'=4] {'ka'}, dimensions={0}, use_global_device_ids=true | all-gather | bytes 245760 | tf_op jit(solution)/shard_map/all_gather | solution.py:40
  30.1 22.2 %all_gather.6 = f32[128,4,96]{2,1,0:T(4,128)S(1)} all-gather(f32[16,4,96]{2,1,0:T(4,128)} %param.10), channel_id=1, replica_groups=mesh['ia'=16,'ja'=8,'ka'=4] {'ja'}, dimensions={0}, use_global_device_ids=true | all-gather | bytes 221184 | tf_op jit(solution)/shard_map/all_gather | solution.py:33
  52.3 0.1 copy.51
  52.4 0.1 copy.52
  52.6 0.1 copy.34
  52.7 1.3 dynamic-slice
  54.0 1.3 dynamic-slice.2
  55.9 0.0 copy-done
  55.9 5.5 %multiply_reduce_fusion = f32[384,32]{0,1:T(8,128)S(1)} fusion(f32[384,128]{0,1:T(8,128)S(1)} %copy.52, f32[32,128,128]{2,1,0:T(8,128)S(1)} %copy-done, f32[128,384,1]{0,1,2:T(8,128)S(1)} %bitcast.141), kind=kOutput, calls=%fused_computation | convolution fusion | flops 2419052544 | bytes 2539520 | tf_op jit(solution)/shard_map/dot_general | solution.py:34
  61.4 23.5 %all-reduce = f32[32,384]{1,0:T(8,128)S(1)} all-reduce(f32[32,384]{1,0:T(8,128)S(1)} %bitcast.142), channel_id=2, replica_groups=mesh['ia'=16,'ja'=8,'ka'=4] {'ja'}, use_global_device_ids=true, to_apply=%region_4.0.clone | all-reduce | flops 12288 | bytes 98304
  84.9 9.5 %all-reduce.1 = f32[4,384]{1,0:T(4,128)S(1)} all-reduce(f32[4,384]{1,0:T(4,128)S(1)} %constant_dynamic-slice_fusion), channel_id=3, replica_groups=mesh['ia'=16,'ja'=8,'ka'=4] {'ka'}, use_global_device_ids=true, to_apply=%region_5.0.clone | all-reduce | flops 1536 | bytes 12288
  94.5 0.7 dynamic-slice_reduce_fusion
  95.1 0.1 reshape.87
  95.2 210.4 %all-reduce.5.cloned.1.call-done = (f32[4,96,96]{1,2,0:T(8,128)}, f32[4,96,96]{1,2,0:T(8,128)}) async-done(((f32[4,96,96]{1,2,0:T(8,128)}, f32[4,96,96]{1,2,0:T(8,128)}), (f32[4,96,96]{1,2,0:T(8,128)}, f32[4,96,96]{1,2,0:T(8,128)})) %all-reduce.5.cloned.1.call-update) | async-done | bytes 294928 | tf_op jit(solution)/shard_map/psum | solution.py:52
  305.6 1.0 fusion.24
  306.6 0.1 copy.33
  306.7 0.1 copy.39
  306.8 0.1 copy.38
  306.9 0.1 copy.37
  307.0 1.0 fusion.9
  308.0 8.8 %cholesky.107 = f32[96,96]{1,0:T(8,128)S(1)} custom-call(f32[96,96]{1,0:T(8,128)S(1)} %get-tuple-element.10), custom_call_target="Cholesky" | custom-call | tf_op jit(solution)/shard_map/jit(cholesky)/cholesky | solution.py:19
  316.8 0.6 compare_reduce_fusion
  317.5 0.7 fusion.5
  318.1 7.4 %custom-call.21 = f32[1,96,96]{1,2,0:T(8,128)S(1)} custom-call(f32[1,96,96]{2,1,0:T(8,128)S(1)} %fusion.5), custom_call_target="InvertDiagBlocksLowerTriangular" | custom-call | tf_op jit(solution)/shard_map/triangular_solve/custom-call.2 | solution.py:22
  325.5 0.1 convolution_bitcast_fusion
  325.6 0.2 fusion.11
  325.8 8.8 %cholesky.96 = f32[96,96]{1,0:T(8,128)S(1)} custom-call(f32[96,96]{1,0:T(8,128)S(1)} %get-tuple-element.11), custom_call_target="Cholesky" | custom-call | tf_op jit(solution)/shard_map/jit(cholesky)/cholesky | solution.py:19
  334.7 0.6 compare_reduce_fusion.1
  335.3 0.7 fusion.4
  336.0 7.4 %custom-call.19 = f32[1,96,96]{1,2,0:T(8,128)S(1)} custom-call(f32[1,96,96]{2,1,0:T(8,128)S(1)} %fusion.4), custom_call_target="InvertDiagBlocksLowerTriangular" | custom-call | tf_op jit(solution)/shard_map/triangular_solve/custom-call.2 | solution.py:22
  343.3 0.1 convolution_bitcast_fusion.1
  343.5 0.2 fusion.14
  343.7 8.8 %cholesky.85 = f32[96,96]{1,0:T(8,128)S(1)} custom-call(f32[96,96]{1,0:T(8,128)S(1)} %get-tuple-element.12), custom_call_target="Cholesky" | custom-call | tf_op jit(solution)/shard_map/jit(cholesky)/cholesky | solution.py:19
  352.5 0.6 compare_reduce_fusion.2
  353.1 0.7 fusion.3
  353.8 7.4 %custom-call.17 = f32[1,96,96]{1,2,0:T(8,128)S(1)} custom-call(f32[1,96,96]{2,1,0:T(8,128)S(1)} %fusion.3), custom_call_target="InvertDiagBlocksLowerTriangular" | custom-call | tf_op jit(solution)/shard_map/triangular_solve/custom-call.2 | solution.py:22
  361.2 0.1 convolution_bitcast_fusion.2
  361.3 0.2 fusion.17
  361.5 9.0 %cholesky.74 = f32[96,96]{1,0:T(8,128)S(1)} custom-call(f32[96,96]{1,0:T(8,128)S(1)} %get-tuple-element.9), custom_call_target="Cholesky" | custom-call | tf_op jit(solution)/shard_map/jit(cholesky)/cholesky | solution.py:19
  370.6 0.6 compare_reduce_fusion.3
  371.2 0.7 fusion.2
  371.9 7.4 %custom-call.15 = f32[1,96,96]{1,2,0:T(8,128)S(1)} custom-call(f32[1,96,96]{2,1,0:T(8,128)S(1)} %fusion.2), custom_call_target="InvertDiagBlocksLowerTriangular" | custom-call | tf_op jit(solution)/shard_map/triangular_solve/custom-call.2 | solution.py:22
  379.2 0.1 convolution_bitcast_fusion.3
  379.4 0.2 fusion.20
  379.6 116.4 %psum.23 = f32[4,96]{1,0:T(4,128)S(1)} all-reduce(f32[4,96]{1,0:T(4,128)S(1)} %fusion.36), channel_id=1, replica_groups=mesh['ia'=16,'ja'=8,'ka'=4] {'ia','ja','ka'}, use_global_device_ids=true, to_apply=%region_6.10 | all-reduce | flops 384 | bytes 3072 | tf_op jit(solution)/shard_map/psum | solution.py:58
  496.0 0.6 divide_bitcast_fusion
  (6 shorter events, 0.2 us)
Async XLA Ops:
  7.2 48.7 %copy-start = (f32[32,128,128]{2,1,0:T(8,128)S(1)}, f32[32,128,128]{2,1,0:T(8,128)}, u32[]{:S(2)}) copy-start(f32[32,128,128]{2,1,0:T(8,128)} %param.8) | copy-start | bytes 6291460
  7.2 298.5 %all-reduce.5.cloned.1.call-start = ((), (), s32[]{:S(2)}) async-start(), calls=%async_computation | async-start | bytes 786432 | tf_op jit(solution)/shard_map/psum | solution.py:52
Sparse Core Ops, SparseCore 0:
  11.5 294.0 all-reduce.4
where the time goes:
time: 504 us; the launch traced here: 503 us
  waiting for transfers between devices  210 us (42%)
  blocking collectives  190 us (38%)
  other arithmetic  72.8 us (14%)
  between operations  14.9 us (3%)
  matrix products  11 us (2%)
    psum x1, waiting for transfers between devices, shards(): lax.psum((gram_of(factor_b), gram_of(factor_c)), ('ja', 'ka'))  210 us
    psum x1, blocking collectives, shards(): total = lax.psum(squares, ('ia', 'ja', 'ka'))  116 us
    another operation x12, other arithmetic, solve_normal(): factor_l = jnp.linalg.cholesky(normal_mat)  38.1 us
    unnamed x2, blocking collectives  33 us
    another operation x8, other arithmetic, solve_normal(): lax.linalg.triangular_solve(factor_l, lower_sol, left_side=True, lower=Tr...  32 us
    all_gather x1, blocking collectives, shards(): c_block = lax.all_gather(factor_c, 'ja', axis=0, tiled=True)  22.2 us
    all_gather x1, blocking collectives, shards(): piece = lax.all_gather(factor_b, 'ka', axis=0, tiled=True)  18.7 us
  transfers between devices with their start and end apart: 1, of which 1 were waited for; matrix products, arithmetic and copies ran while one was open for 2% of the time, Pallas kernels for 0%

commit v1 on v0

--- a/solution.py
+++ b/solution.py
@@ -4,6 +4,13 @@
 from jax.sharding import PartitionSpec as P
 
 highest = lax.Precision.HIGHEST
+
+
+def swapped_in(x, axis, along):
+    n_dev = lax.axis_size(axis)
+    blocks = jnp.stack([x for _ in range(n_dev)])
+    blocks = lax.all_to_all(blocks, axis, split_axis=0, concat_axis=0)
+    return jnp.concatenate(blocks, axis=along)
 
 
 def gram_of(rows):
@@ -37,7 +44,7 @@
         precision=highest,
         preferred_element_type=jnp.float32,
     ).reshape(rows_i, rows_j, width)
-    piece = lax.all_gather(factor_b, "ka", axis=0, tiled=True)
+    piece = swapped_in(factor_b, "ka", 0)
     gram_sum = jnp.zeros((starts, col_count, col_count), jnp.float32)
     count = piece.shape[0]
     flat_rows = piece.reshape(count, width)

time: 504 us -> 549 us (1.089)
  waiting for transfers between devices: 210 us -> 256 us
  blocking collectives: 190 us -> 177 us
  starting transfers between devices: 0.04 us -> 10.9 us
    psum x1, waiting for transfers between devices: 210 us -> 256 us  [shards(): lax.psum((gram_of(factor_b), gram_of(factor_c)), ('ja', 'ka'))]
    all_gather x1 -> x0, blocking collectives: 18.7 us -> none  [shards(): piece = lax.all_gather(factor_b, 'ka', axis=0, tiled=True)]
    all_to_all x0 -> x1, starting transfers between devices: none -> 10.8 us  [swapped_in(): blocks = lax.all_to_all(blocks, axis, split_axis=0, concat_axis=0)]
    psum x1, blocking collectives: 116 us -> 125 us  [shards(): total = lax.psum(squares, ('ia', 'ja', 'ka'))]
  transfers between devices with their start and end apart: 1 -> 2, of which waited for: 1 -> 1; matrix products, arithmetic and copies ran while one was open for 2% -> 4% of each run, Pallas kernels for 0% -> 0%
where the time goes in v1:
time: 549 us; the launch traced here: 548 us
  waiting for transfers between devices  256 us (47%)
  blocking collectives  177 us (32%)
  other arithmetic  72.6 us (13%)
  between operations  14.9 us (3%)
  matrix products  11 us (2%)
  starting transfers between devices  10.9 us (2%)
  local copies, waits for them, and re-layouts  5.5 us (1%)
    psum x1, waiting for transfers between devices, shards(): lax.psum((gram_of(factor_b), gram_of(factor_c)), ('ja', 'ka'))  256 us
    psum x1, blocking collectives, shards(): total = lax.psum(squares, ('ia', 'ja', 'ka'))  125 us
    another operation x12, other arithmetic, solve_normal(): factor_l = jnp.linalg.cholesky(normal_mat)  37.9 us
    another operation x8, other arithmetic, solve_normal(): lax.linalg.triangular_solve(factor_l, lower_sol, left_side=True, lower=Tr...  32 us
    unnamed x2, blocking collectives  30 us
    all_gather x1, blocking collectives, shards(): c_block = lax.all_gather(factor_c, 'ja', axis=0, tiled=True)  21.9 us
  transfers between devices with their start and end apart: 2, of which 1 were waited for; matrix products, arithmetic and copies ran while one was open for 4% of the time, Pallas kernels for 0%

profile of v1, /device:TPU:1, one launch (start us, length us, event | category | flops | bytes accessed | tf_op | source)
XLA Modules:
  0.0 548.2 jit_solution(10203331546459965260)
XLA Ops:
  7.2 0.0 copy-start
  7.2 0.0 all-reduce.5.cloned.1.call-start
  7.2 2.1 fusion.22
  9.3 2.1 fusion
  11.4 0.0 all-reduce.5.cloned.1.call-update
  11.4 1.6 stack.18
  13.0 10.8 %all-to-all-start = ((f32[4,32,4,96]{3,2,1,0:T(4,128)}), f32[4,32,4,96]{3,2,1,0:T(4,128)S(1)}, u32[]{:S(2)}, u32[]{:S(2)}) async-start(f32[4,32,4,96]{3,2,1,0:T(4,128)} %stack.18), calls=%async_computation | async-start | bytes 524288 | tf_op jit(solution)/shard_map/all_to_all | solution.py:12
  23.8 21.9 %all_gather.3 = f32[128,4,96]{2,1,0:T(4,128)S(1)} all-gather(f32[16,4,96]{2,1,0:T(4,128)} %param.10), channel_id=1, replica_groups=mesh['ia'=16,'ja'=8,'ka'=4] {'ja'}, dimensions={0}, use_global_device_ids=true | all-gather | bytes 221184 | tf_op jit(solution)/shard_map/all_gather | solution.py:40
  45.7 0.1 copy.33
  45.9 1.3 dynamic-slice
  47.1 1.3 dynamic-slice.2
  49.1 256.5 %all-reduce.5.cloned.1.call-done = (f32[4,96,96]{1,2,0:T(8,128)}, f32[4,96,96]{1,2,0:T(8,128)}) async-done(((f32[4,96,96]{1,2,0:T(8,128)}, f32[4,96,96]{1,2,0:T(8,128)}), (f32[4,96,96]{1,2,0:T(8,128)}, f32[4,96,96]{1,2,0:T(8,128)})) %all-reduce.5.cloned.1.call-update) | async-done | bytes 294928 | tf_op jit(solution)/shard_map/psum | solution.py:59
  305.5 1.0 fusion.24
  306.5 0.1 copy.32
  306.6 0.1 copy.37
  306.7 0.1 copy.36
  306.8 0.1 copy.35
  306.9 1.0 fusion.9
  307.9 8.8 %cholesky.107 = f32[96,96]{1,0:T(8,128)S(1)} custom-call(f32[96,96]{1,0:T(8,128)S(1)} %get-tuple-element.10), custom_call_target="Cholesky" | custom-call | tf_op jit(solution)/shard_map/jit(cholesky)/cholesky | solution.py:26
  316.7 0.6 compare_reduce_fusion
  317.4 0.7 fusion.5
  318.0 7.4 %custom-call.21 = f32[1,96,96]{1,2,0:T(8,128)S(1)} custom-call(f32[1,96,96]{2,1,0:T(8,128)S(1)} %fusion.5), custom_call_target="InvertDiagBlocksLowerTriangular" | custom-call | tf_op jit(solution)/shard_map/triangular_solve/custom-call.2 | solution.py:29
  325.4 0.0 all-to-all-done
  325.4 0.2 reshape_reshape.3
  325.6 0.0 copy-done
  325.6 5.5 %multiply_reduce_fusion = f32[384,32]{0,1:T(8,128)S(1)} fusion(f32[384,128]{0,1:T(8,128)S(1)} %bitcast.138, f32[32,128,128]{2,1,0:T(8,128)S(1)} %copy-done, f32[128,384,1]{0,1,2:T(8,128)S(1)} %bitcast.137), kind=kOutput, calls=%fused_computation | convolution fusion | flops 2419052544 | bytes 2539520 | tf_op jit(solution)/shard_map/dot_general | solution.py:41
  331.1 20.5 %all-reduce = f32[32,384]{1,0:T(8,128)S(1)} all-reduce(f32[32,384]{1,0:T(8,128)S(1)} %bitcast.139), channel_id=2, replica_groups=mesh['ia'=16,'ja'=8,'ka'=4] {'ja'}, use_global_device_ids=true, to_apply=%region_4.0.clone | all-reduce | flops 12288 | bytes 98304
  351.6 9.5 %all-reduce.1 = f32[4,384]{1,0:T(4,128)S(1)} all-reduce(f32[4,384]{1,0:T(4,128)S(1)} %constant_dynamic-slice_fusion), channel_id=3, replica_groups=mesh['ia'=16,'ja'=8,'ka'=4] {'ka'}, use_global_device_ids=true, to_apply=%region_5.0.clone | all-reduce | flops 1536 | bytes 12288
  361.1 0.7 dynamic-slice_reduce_fusion
  361.8 0.1 reshape.85
  361.8 0.1 convolution_bitcast_fusion
  362.0 0.2 fusion.11
  362.2 8.8 %cholesky.96 = f32[96,96]{1,0:T(8,128)S(1)} custom-call(f32[96,96]{1,0:T(8,128)S(1)} %get-tuple-element.11), custom_call_target="Cholesky" | custom-call | tf_op jit(solution)/shard_map/jit(cholesky)/cholesky | solution.py:26
  371.0 0.6 compare_reduce_fusion.1
  371.7 0.7 fusion.4
  372.3 7.4 %custom-call.19 = f32[1,96,96]{1,2,0:T(8,128)S(1)} custom-call(f32[1,96,96]{2,1,0:T(8,128)S(1)} %fusion.4), custom_call_target="InvertDiagBlocksLowerTriangular" | custom-call | tf_op jit(solution)/shard_map/triangular_solve/custom-call.2 | solution.py:29
  379.7 0.1 convolution_bitcast_fusion.1
  379.8 0.2 fusion.14
  380.0 8.8 %cholesky.85 = f32[96,96]{1,0:T(8,128)S(1)} custom-call(f32[96,96]{1,0:T(8,128)S(1)} %get-tuple-element.12), custom_call_target="Cholesky" | custom-call | tf_op jit(solution)/shard_map/jit(cholesky)/cholesky | solution.py:26
  388.9 0.6 compare_reduce_fusion.2
  389.5 0.7 fusion.3
  390.2 7.4 %custom-call.17 = f32[1,96,96]{1,2,0:T(8,128)S(1)} custom-call(f32[1,96,96]{2,1,0:T(8,128)S(1)} %fusion.3), custom_call_target="InvertDiagBlocksLowerTriangular" | custom-call | tf_op jit(solution)/shard_map/triangular_solve/custom-call.2 | solution.py:29
  397.5 0.1 convolution_bitcast_fusion.2
  397.7 0.2 fusion.17
  397.9 8.8 %cholesky.74 = f32[96,96]{1,0:T(8,128)S(1)} custom-call(f32[96,96]{1,0:T(8,128)S(1)} %get-tuple-element.9), custom_call_target="Cholesky" | custom-call | tf_op jit(solution)/shard_map/jit(cholesky)/cholesky | solution.py:26
  406.7 0.6 compare_reduce_fusion.3
  407.4 0.7 fusion.2
  408.0 7.4 %custom-call.15 = f32[1,96,96]{1,2,0:T(8,128)S(1)} custom-call(f32[1,96,96]{2,1,0:T(8,128)S(1)} %fusion.2), custom_call_target="InvertDiagBlocksLowerTriangular" | custom-call | tf_op jit(solution)/shard_map/triangular_solve/custom-call.2 | solution.py:29
  415.4 0.1 convolution_bitcast_fusion.3
  415.5 0.2 fusion.20
  415.8 125.0 %psum.23 = f32[4,96]{1,0:T(4,128)S(1)} all-reduce(f32[4,96]{1,0:T(4,128)S(1)} %fusion.36), channel_id=1, replica_groups=mesh['ia'=16,'ja'=8,'ka'=4] {'ia','ja','ka'}, use_global_device_ids=true, to_apply=%region_6.10 | all-reduce | flops 384 | bytes 3072 | tf_op jit(solution)/shard_map/psum | solution.py:65
  540.8 0.6 divide_bitcast_fusion
  (6 shorter events, 0.2 us)
Async XLA Ops:
  7.2 318.4 %copy-start = (f32[32,128,128]{2,1,0:T(8,128)S(1)}, f32[32,128,128]{2,1,0:T(8,128)}, u32[]{:S(2)}) copy-start(f32[32,128,128]{2,1,0:T(8,128)} %param.8) | copy-start | bytes 6291460
  7.2 298.4 %all-reduce.5.cloned.1.call-start = ((), (), s32[]{:S(2)}) async-start(), calls=%async_computation.1 | async-start | bytes 786432 | tf_op jit(solution)/shard_map/psum | solution.py:59
  13.0 312.4 %all-to-all-start = ((f32[4,32,4,96]{3,2,1,0:T(4,128)}), f32[4,32,4,96]{3,2,1,0:T(4,128)S(1)}, u32[]{:S(2)}, u32[]{:S(2)}) async-start(f32[4,32,4,96]{3,2,1,0:T(4,128)} %stack.18), calls=%async_computation | async-start | bytes 524288 | tf_op jit(solution)/shard_map/all_to_all | solution.py:12
Sparse Core Ops, SparseCore 0:
  11.5 293.9 all-reduce.4
